TPU v7x, 32 devices: a whole 2x2x4 slice. The times are simulated.
32 devices in a mesh: span: 4 (over z), space: 8 (over y, x, core).
Axes of the slice: x: 2, y: 2, z: 4, core: 2. Of those that a mesh axis runs over, the one named last changes fastest.
Arguments:
- frames: bfloat16 [12, 8, 32, 512], P('span', 'space')
- counts: int32 [4], replicated, may hold values from 1 to 3, as said below
- gain_one: float32 [512], replicated, may hold values from 0.5 to 1.5
- offset_one: float32 [512], replicated, may hold values from -3 to 3
- kernel_one: bfloat16 [3, 3, 3, 512, 512], P(None, None, None, 'space'), may hold values from -0.0546875 to 0.0546875
- bias_one: float32 [512], replicated, may hold values from -2 to 2
- gain_two: float32 [512], replicated, may hold values from 0.5 to 1.5
- offset_two: float32 [512], replicated, may hold values from -3 to 3
- kernel_two: bfloat16 [3, 3, 3, 512, 512], P(None, None, None, 'space'), may hold values from -0.0546875 to 0.0546875
- bias_two: float32 [512], replicated, may hold values from -2 to 2
Outputs:
- decoded: bfloat16 [12, 8, 32, 512], P('span', 'space')
Inputs may be any that keep to these rules, and one draw needn't show every extreme that they name: `counts`: each group's live frames fill its first slots; some group is full and some group has one live frame.
All inputs are finite; a program needn't handle non-finite values.
Results may differ from a plain program's by a relative error of at most 0.003.
Values may be sent and summed in bfloat16 or wider, within the bound.
A program may use at most 64 MiB of HBM per device.

v0:
```python
import jax
import jax.numpy as jnp
from jax import lax
from jax.sharding import PartitionSpec as P

GROUPS = 32


EPS = 1e-05


def entering(part, axis, combine, identity):
    place = lax.axis_index(axis)
    gathered = jax.tree.map(lambda a: lax.all_gather(a, axis), part)
    state = jax.tree.map(lambda a, e: jnp.zeros_like(a) + jnp.asarray(e, a.dtype), part, identity)

    def one(hop, state):
        return combine(
            state, jax.tree.map(lambda a: lax.dynamic_index_in_dim(a, hop, 0, False), gathered)
        )

    return lax.fori_loop(0, place, one, state)


def group_sums(values, groups_here):
    grouped = values.astype(jnp.float32).reshape(
        values.shape[0], values.shape[1], values.shape[2], groups_here, -1
    )
    return (jnp.sum(grouped, axis=(1, 2, 4)), jnp.sum(grouped * grouped, axis=(1, 2, 4)))


def apply_norm(values, group_total, squares, members, gain_vec, offset_vec, live_mask):
    groups_here = group_total.shape[1]
    grouped = values.astype(jnp.float32).reshape(
        values.shape[0], values.shape[1], values.shape[2], groups_here, -1
    )
    average = group_total / members
    spread = squares / members - average * average
    scale_now = lax.rsqrt(spread + EPS)
    normed = (grouped - average[:, None, None, :, None]) * scale_now[:, None, None, :, None]
    normed = normed.reshape(values.shape) * gain_vec + offset_vec
    return (jax.nn.silu(normed) * live_mask[:, None, None, None]).astype(jnp.bfloat16)


def own_cache(values, count_now):
    padded = jnp.concatenate([jnp.zeros((2,) + values.shape[1:], jnp.bfloat16), values], 0)
    return lax.dynamic_slice_in_dim(padded, count_now, 2, 0)


def merge_cache(early_state, later_state):
    early_frames, early_count = early_state
    later_frames, later_count = later_state
    padded = jnp.concatenate([early_frames, jnp.zeros_like(early_frames)], 0)
    shifted = lax.dynamic_slice_in_dim(padded, later_count.astype(jnp.int32), 2, 0)
    merged_count = jnp.minimum(early_count + later_count, 2.0).astype(jnp.bfloat16)
    return (shifted + later_frames, merged_count)


def spread_taps(stacked, kernel, frames_out):
    row_count = stacked.shape[1]
    col_count = stacked.shape[2]
    channels = stacked.shape[3]
    out_width = kernel.shape[3]
    padded = jnp.pad(stacked, ((0, 0), (1, 1), (1, 1), (0, 0)))
    summed = jnp.zeros((frames_out, row_count, col_count, out_width), jnp.float32)
    for time_off in range(3):
        window = padded[time_off : time_off + frames_out]
        matrix = kernel[time_off].reshape(9 * out_width, channels)
        tap_terms = lax.dot_general(
            window.reshape(-1, channels),
            matrix,
            (((1,), (1,)), ((), ())),
            preferred_element_type=jnp.float32,
        )
        tap_terms = tap_terms.reshape(frames_out, row_count + 2, col_count + 2, 9, out_width)
        for row_off in range(3):
            for col_off in range(3):
                summed = (
                    summed
                    + tap_terms[
                        :,
                        row_off : row_off + row_count,
                        col_off : col_off + col_count,
                        row_off * 3 + col_off,
                    ]
                )
    return summed


def per_device(
    frames,
    counts,
    gain_one,
    offset_one,
    kernel_one,
    bias_one,
    gain_two,
    offset_two,
    kernel_two,
    bias_two,
):
    frame_slots = frames.shape[0]
    group_index = lax.axis_index("span")
    count_now = lax.dynamic_index_in_dim(counts, group_index, keepdims=False)
    live_mask = (jnp.arange(frame_slots) < count_now).astype(jnp.float32)
    devices = lax.axis_size("space")
    width_out = kernel_one.shape[3]
    channel_start = lax.axis_index("space") * width_out
    members = frames.shape[1] * devices * frames.shape[2] * (frames.shape[3] // GROUPS)
    count_wire = jnp.minimum(count_now, 2).astype(jnp.bfloat16)
    group_total, squares = group_sums(frames, GROUPS)
    group_total, squares = lax.psum((group_total, squares), "space")
    normed_one = apply_norm(frames, group_total, squares, members, gain_one, offset_one, live_mask)
    empty_one = (jnp.zeros((2,) + normed_one.shape[1:], jnp.bfloat16), jnp.zeros((), jnp.bfloat16))
    cache_one, unused_one = entering(
        (own_cache(normed_one, count_now), count_wire), "span", merge_cache, empty_one
    )
    stacked_one = jnp.concatenate([cache_one, normed_one], 0)
    full_one = lax.all_gather(stacked_one, "space", axis=1, tiled=True)
    conv_one = spread_taps(full_one, kernel_one, frame_slots) + lax.dynamic_slice_in_dim(
        bias_one, channel_start, width_out
    )
    conv_one = conv_one.astype(jnp.bfloat16)
    hidden_mixed = lax.all_to_all(conv_one, "space", split_axis=1, concat_axis=3, tiled=True)
    total_two, squares_two = group_sums(hidden_mixed, GROUPS)
    total_two, squares_two = lax.psum((total_two, squares_two), "space")
    normed_two = apply_norm(
        hidden_mixed, total_two, squares_two, members, gain_two, offset_two, live_mask
    )
    empty_two = (jnp.zeros((2,) + normed_two.shape[1:], jnp.bfloat16), jnp.zeros((), jnp.bfloat16))
    cache_two, unused_two = entering(
        (own_cache(normed_two, count_now), count_wire), "span", merge_cache, empty_two
    )
    stacked_two = jnp.concatenate([cache_two, normed_two], 0)
    full_two = lax.all_gather(stacked_two, "space", axis=1, tiled=True)
    conv_two = spread_taps(full_two, kernel_two, frame_slots) + lax.dynamic_slice_in_dim(
        bias_two, channel_start, width_out
    )
    conv_two = conv_two.astype(jnp.bfloat16)
    returned = lax.all_to_all(conv_two, "space", split_axis=1, concat_axis=3, tiled=True)
    decoded = (frames.astype(jnp.float32) + returned.astype(jnp.float32)) * live_mask[
        :, None, None, None
    ]
    return decoded.astype(jnp.bfloat16)


def solution(mesh):
    return jax.shard_map(
        per_device,
        mesh=mesh,
        in_specs=(
            P("span", "space", None, None),
            P(),
            P(),
            P(),
            P(None, None, None, "space", None),
            P(),
            P(),
            P(),
            P(None, None, None, "space", None),
            P(),
        ),
        out_specs=P("span", "space", None, None),
        check_vma=False,
    )
```

profile of v0, /device:TPU:25, one launch (start us, length us, event | category | flops | bytes accessed | tf_op | source)
XLA Modules:
  0.0 178.5 jit_solution(14932574321147831700)
XLA Ops:
  6.5 1.4 dynamic_slice.42
  8.6 0.6 compare_convert_fusion
  9.9 0.9 convert_reduce_fusion
  10.8 0.1 reduce_sum.47
  10.9 0.1 reduce_sum.53
  11.0 0.1 reduce_sum.51
  11.1 0.1 reduce_sum.54
  11.2 11.8 %all-reduce.8 = (f32[3,32]{1,0:T(4,128)S(1)}, f32[3,32]{1,0:T(4,128)S(1)}) all-reduce(f32[3,32]{1,0:T(4,128)S(1)} %reduce_sum.54, f32[3,32]{1,0:T(4,128)S(1)} %reduce_sum.51), channel_id=1, replica_groups=mesh['span'=4,'space'=8] {'space'}, use_global_device_ids=true, to_apply=%region_5.6 | all-reduce | flops 192 | bytes 1536 | tf_op jit(solution)/shard_map/psum | solution.py:112
  23.0 0.1 mul.134
  23.1 0.1 mul.135
  23.2 0.1 sub.44
  23.3 0.1 sub.45
  24.0 1.0 fusion.55
  25.1 11.4 %all-gather = bf16[8,1,32,512]{3,2,1,0:T(8,128)(2,1)S(1)} all-gather(bf16[2,1,32,512]{3,2,1,0:T(8,128)(2,1)S(1)} %pad_dynamic-slice_fusion.3), channel_id=2, replica_groups=mesh['span'=4,'space'=8] {'span'}, dimensions={0}, use_global_device_ids=true | all-gather | bytes 327680 | tf_op jit(solution)/shard_map/all_gather | solution.py:14
  37.2 1.3 dynamic-slice
  38.5 0.8 dynamic-update-slice
  39.3 6.4 %all-reduce.6 = bf16[4]{0:T(256)(128)(2,1)S(1)} all-reduce(bf16[4]{0:T(256)(128)(2,1)S(1)} %dynamic-update-slice), channel_id=1, replica_groups=mesh['span'=4,'space'=8] {'span'}, use_global_device_ids=true, to_apply=%add.6 | all-reduce | flops 4 | bytes 16
  45.7 4.4 %while.24 = (s32[]{:T(128)}, bf16[2,1,32,512]{3,2,1,0:T(8,128)(2,1)S(1)}, s32[]{:T(128)}, bf16[4]{0:T(256)(128)(2,1)S(1)}, bf16[4,2,1,32,512]{4,3,1,2,0:T(8,128)(2,1)S(1)}, /*index=5*/s32[]{:T(128)}, s32[]{:T(128)}, s32[]{:T(128)}) while((s32[]{:T(128)}, bf16[2,1,32,512]{3,2,1,0:T(8,128)(2,1)S(1)}, s32[]{:T(128)}, bf16[4]{0:T(256)(128)(2,1)S(1)}, ...), condition=%wide.region_7.8_spmd, body=%wide.region_6.7_spmd.sunk | while | flops 32777 | bytes 327855 | solution.py:22
  45.7 0.7 dynamic_slice.65
  47.1 0.7 dynamic_slice.65
  48.6 0.7 dynamic_slice.65
  50.0 0.7 pad_maximum_fusion
  50.7 0.8 dynamic_slice.44
  51.5 0.2 fusion.67
  51.7 29.4 %all-gather.5.cloned.1.call-done = bf16[5,8,32,512]{3,2,1,0:T(8,128)(2,1)} async-done(((bf16[5,1,32,512]{3,2,1,0:T(8,128)(2,1)}), bf16[5,8,32,512]{3,2,1,0:T(8,128)(2,1)}) %all-gather.5.cloned.1.call-update) | async-done | bytes 1310736 | tf_op jit(solution)/shard_map/all_gather | solution.py:119
  81.1 3.0 %fusion.3 = f32[3,10,34,9,64]{4,2,3,1,0:T(8,128)S(1)} fusion(bf16[9,64,512,1,1]{2,1,0,4,3:T(8,128)(2,1)S(1)} %bitcast.284, bf16[5,8,32,512]{3,2,1,0:T(8,128)(2,1)} %all-gather.5.cloned.1.call-done), kind=kOutput, calls=%fused_computation.11 | convolution fusion | flops 601620480 | bytes 4250624 | tf_op jit(solution)/shard_map/dot_general | solution.py:69
  84.1 1.8 %fusion.6 = f32[3,10,34,9,64]{4,2,3,1,0:T(8,128)S(1)} fusion(bf16[9,64,512,1,1]{2,1,0,4,3:T(8,128)(2,1)S(1)} %bitcast.282, bf16[5,8,32,512]{3,2,1,0:T(8,128)(2,1)S(1)} %copy-done.5), kind=kOutput, calls=%fused_computation.13 | convolution fusion | flops 601620480 | bytes 4250624 | tf_op jit(solution)/shard_map/dot_general | solution.py:69
  85.9 1.8 %fusion.9 = f32[3,10,34,9,64]{4,2,1,0,3:T(8,128)S(1)} fusion(bf16[9,64,512,1,1]{2,1,4,3,0:T(8,128)(2,1)S(1)} %bitcast.280, bf16[5,8,32,512]{3,2,1,0:T(8,128)(2,1)S(1)} %copy-done.5), kind=kOutput, calls=%fused_computation.15 | convolution fusion | flops 601620480 | bytes 4250624 | tf_op jit(solution)/shard_map/dot_general | solution.py:69
  87.7 1.2 copy_bitcast_fusion.1
  88.9 0.8 reshape.253
  89.7 3.5 %all-to-all-start = ((bf16[8,2,3072]{2,1,0:T(2,128)(2,1)}), bf16[8,2,3072]{2,1,0:T(2,128)(2,1)S(1)}, u32[]{:S(2)}, u32[]{:S(2)}) async-start(bf16[8,2,3072]{2,1,0:T(2,128)(2,1)} %reshape.253), calls=%async_computation | async-start | bytes 196608 | tf_op jit(solution)/shard_map/all_to_all | solution.py:124
  93.2 4.3 %all-to-all-done = bf16[8,2,3072]{2,1,0:T(2,128)(2,1)S(1)} async-done(((bf16[8,2,3072]{2,1,0:T(2,128)(2,1)}), bf16[8,2,3072]{2,1,0:T(2,128)(2,1)S(1)}, u32[]{:S(2)}, u32[]{:S(2)}) %all-to-all-start) | async-done | bytes 98336 | tf_op jit(solution)/shard_map/all_to_all | solution.py:124
  97.5 0.2 reshape.254
  97.7 0.1 fusion.59
  97.9 0.1 reduce_sum.59
  98.0 0.1 reduce_sum.72
  98.1 0.1 reduce_sum.74
  98.1 0.1 reduce_sum.75
  98.2 12.1 %all-reduce.7 = (f32[3,32]{1,0:T(4,128)S(1)}, f32[3,32]{1,0:T(4,128)S(1)}) all-reduce(f32[3,32]{1,0:T(4,128)S(1)} %reduce_sum.75, f32[3,32]{1,0:T(4,128)S(1)} %reduce_sum.72), channel_id=1, replica_groups=mesh['span'=4,'space'=8] {'space'}, use_global_device_ids=true, to_apply=%region_13.14 | all-reduce | flops 192 | bytes 1536 | tf_op jit(solution)/shard_map/psum | solution.py:126
  110.3 0.1 mul.146
  110.4 0.1 mul.147
  110.6 0.1 sub.50
  110.7 0.2 copy.97
  111.0 0.1 reshape.206
  111.1 0.1 multiply_convert_fusion
  111.2 11.2 %all-gather.1 = bf16[8,1,32,512]{3,2,1,0:T(8,128)(2,1)S(1)} all-gather(bf16[2,1,32,512]{3,2,1,0:T(8,128)(2,1)S(1)} %pad_dynamic-slice_fusion.2), channel_id=3, replica_groups=mesh['span'=4,'space'=8] {'span'}, dimensions={0}, use_global_device_ids=true | all-gather | bytes 327680 | tf_op jit(solution)/shard_map/all_gather | solution.py:14
  122.5 4.1 %while.25 = (s32[]{:T(128)}, bf16[2,1,32,512]{3,2,1,0:T(8,128)(2,1)S(1)}, s32[]{:T(128)}, bf16[4]{0:T(256)(128)(2,1)S(1)}, bf16[4,2,1,32,512]{4,3,1,2,0:T(8,128)(2,1)S(1)}, /*index=5*/s32[]{:T(128)}, s32[]{:T(128)}, s32[]{:T(128)}) while((s32[]{:T(128)}, bf16[2,1,32,512]{3,2,1,0:T(8,128)(2,1)S(1)}, s32[]{:T(128)}, ...), condition=%wide.region_15.16_spmd, body=%wide.region_14.15_spmd.sunk | while | flops 32777 | bytes 327855 | solution.py:22
  122.5 0.6 dynamic_slice.68
  123.8 0.6 dynamic_slice.68
  125.1 0.6 dynamic_slice.68
  126.6 0.7 pad_maximum_fusion.1
  127.3 0.8 dynamic_slice.46
  128.1 0.2 fusion.66
  128.3 27.0 %all-gather.7.cloned.1.call-done = bf16[5,8,32,512]{3,2,1,0:T(8,128)(2,1)} async-done(((bf16[5,1,32,512]{3,2,1,0:T(8,128)(2,1)}), bf16[5,8,32,512]{3,2,1,0:T(8,128)(2,1)}) %all-gather.7.cloned.1.call-update) | async-done | bytes 1310736 | tf_op jit(solution)/shard_map/all_gather | solution.py:135
  155.3 3.0 %fusion.12 = f32[3,10,34,9,64]{4,2,3,1,0:T(8,128)S(1)} fusion(bf16[9,64,512,1,1]{2,1,0,4,3:T(8,128)(2,1)S(1)} %bitcast.285, bf16[5,8,32,512]{3,2,1,0:T(8,128)(2,1)} %all-gather.7.cloned.1.call-done), kind=kOutput, calls=%fused_computation.17 | convolution fusion | flops 601620480 | bytes 4250624 | tf_op jit(solution)/shard_map/dot_general | solution.py:69
  158.3 1.8 %fusion.15 = f32[3,10,34,9,64]{4,2,3,1,0:T(8,128)S(1)} fusion(bf16[9,64,512,1,1]{2,1,0,4,3:T(8,128)(2,1)S(1)} %bitcast.283, bf16[5,8,32,512]{3,2,1,0:T(8,128)(2,1)S(1)} %copy-done.6), kind=kOutput, calls=%fused_computation.19 | convolution fusion | flops 601620480 | bytes 4250624 | tf_op jit(solution)/shard_map/dot_general | solution.py:69
  160.1 1.8 %fusion.18 = f32[3,10,34,9,64]{4,2,1,0,3:T(8,128)S(1)} fusion(bf16[9,64,512,1,1]{2,1,4,3,0:T(8,128)(2,1)S(1)} %bitcast.281, bf16[5,8,32,512]{3,2,1,0:T(8,128)(2,1)S(1)} %copy-done.6), kind=kOutput, calls=%fused_computation.21 | convolution fusion | flops 601620480 | bytes 4250624 | tf_op jit(solution)/shard_map/dot_general | solution.py:69
  161.9 1.2 copy_bitcast_fusion
  163.1 0.2 reshape.255
  163.3 7.0 %all_to_all.8 = bf16[8,2,3072]{2,1,0:T(2,128)(2,1)S(1)} all-to-all(bf16[8,2,3072]{2,1,0:T(2,128)(2,1)S(1)} %reshape.255), channel_id=1, replica_groups=mesh['span'=4,'space'=8] {'space'}, dimensions={0} | all-to-all | bytes 196608 | tf_op jit(solution)/shard_map/all_to_all | solution.py:140
  170.3 0.2 reshape.256
  170.6 0.2 copy.112
  170.8 0.1 reshape.208
  170.9 0.7 fusion.58
  (42 shorter events, 0.5 us)
Async XLA Ops:
  6.5 45.0 %copy-start = (bf16[3,3,3,64,512]{4,3,2,1,0:T(8,128)(2,1)S(1)}, bf16[3,3,3,64,512]{4,3,2,1,0:T(8,128)(2,1)}, u32[]{:S(2)}) copy-start(bf16[3,3,3,64,512]{4,3,2,1,0:T(8,128)(2,1)} %param.18) | copy-start | bytes 5308420
  6.5 74.5 %all-gather.5.cloned.1.call-start = ((), (), s32[]{:S(2)}) async-start(), calls=%async_computation.2 | async-start | bytes 1474560 | tf_op jit(solution)/shard_map/all_gather | solution.py:119
  81.1 3.0 %copy-start.5 = (bf16[5,8,32,512]{3,2,1,0:T(8,128)(2,1)S(1)}, bf16[5,8,32,512]{3,2,1,0:T(8,128)(2,1)}, u32[]{:S(2)}) copy-start(bf16[5,8,32,512]{3,2,1,0:T(8,128)(2,1)} %all-gather.5.cloned.1.call-done) | copy-start | bytes 3932164
  88.9 22.2 %copy-start.3 = (f32[512]{0:T(512)S(1)}, f32[512]{0:T(512)}, u32[]{:S(2)}) copy-start(f32[512]{0:T(512)} %param.21) | copy-start | bytes 6148
  88.9 22.2 %copy-start.4 = (f32[512]{0:T(512)S(1)}, f32[512]{0:T(512)}, u32[]{:S(2)}) copy-start(f32[512]{0:T(512)} %param.20) | copy-start | bytes 6148
  89.7 7.8 %all-to-all-start = ((bf16[8,2,3072]{2,1,0:T(2,128)(2,1)}), bf16[8,2,3072]{2,1,0:T(2,128)(2,1)S(1)}, u32[]{:S(2)}, u32[]{:S(2)}) async-start(bf16[8,2,3072]{2,1,0:T(2,128)(2,1)} %reshape.253), calls=%async_computation | async-start | bytes 196608 | tf_op jit(solution)/shard_map/all_to_all | solution.py:124
  93.2 62.0 %all-gather.7.cloned.1.call-start = ((), (), s32[]{:S(2)}) async-start(), calls=%async_computation.3 | async-start | bytes 1474560 | tf_op jit(solution)/shard_map/all_gather | solution.py:135
  110.9 17.1 %copy-start.1 = (bf16[3,3,3,64,512]{4,3,2,1,0:T(8,128)(2,1)S(1)}, bf16[3,3,3,64,512]{4,3,2,1,0:T(8,128)(2,1)}, u32[]{:S(2)}) copy-start(bf16[3,3,3,64,512]{4,3,2,1,0:T(8,128)(2,1)} %param.22) | copy-start | bytes 5308420
  155.3 3.0 %copy-start.6 = (bf16[5,8,32,512]{3,2,1,0:T(8,128)(2,1)S(1)}, bf16[5,8,32,512]{3,2,1,0:T(8,128)(2,1)}, u32[]{:S(2)}) copy-start(bf16[5,8,32,512]{3,2,1,0:T(8,128)(2,1)} %all-gather.7.cloned.1.call-done) | copy-start | bytes 3932164
  163.1 7.8 %copy-start.2 = (bf16[3,1,32,512]{3,2,1,0:T(8,128)(2,1)S(1)}, bf16[3,1,32,512]{3,2,1,0:T(8,128)(2,1)}, u32[]{:S(2)}) copy-start(bf16[3,1,32,512]{3,2,1,0:T(8,128)(2,1)} %param.14) | copy-start | bytes 294916
Sparse Core Ops, SparseCore 0:
  50.9 30.1 all-gather.4
  127.4 27.7 all-gather.6
where the time goes:
time: 181 us; the launch traced here: 179 us
  waiting for transfers between devices  60.7 us (34%)
  blocking collectives  60 us (33%)
  between operations  16.3 us (9%)
  matrix products  13.3 us (7%)
  local copies, waits for them, and re-layouts  12.3 us (7%)
  other arithmetic  7.91 us (4%)
  loops' own time  4.51 us (2%)
  starting transfers between devices  3.5 us (2%)
    all_gather x1, waiting for transfers between devices, per_device(): full_one = lax.all_gather(stacked_one, 'space', axis=1, tiled=True)  29.4 us
    all_gather x1, waiting for transfers between devices, per_device(): full_two = lax.all_gather(stacked_two, 'space', axis=1, tiled=True)  27 us
    all_gather x2, blocking collectives, entering(): gathered = jax.tree.map(lambda a: lax.all_gather(a, axis), part)  22.6 us
    dot_general x6, matrix products, spread_taps(): lax.dot_general(window.reshape(-1, channels), matrix, (((1,), (1,)), ((),...  13.3 us
    psum x1, blocking collectives, per_device(): total_two, squares_two = lax.psum((total_two, squares_two), 'space')  12.1 us
    psum x1, blocking collectives, per_device(): group_total, squares = lax.psum((group_total, squares), 'space')  11.8 us
    all_to_all x1, blocking collectives, per_device(): lax.all_to_all(conv_two, 'space', split_axis=1, concat_axis=3, tiled=True)  7.04 us
    unnamed x1, blocking collectives  6.36 us
  transfers between devices with their start and end apart: 3, of which 3 were waited for; matrix products, arithmetic and copies ran while one was open for 1% of the time, Pallas kernels for 0%

commit v1 on v0

v1 whole, which is shorter than its diff:
```python
import functools

import jax
import jax.numpy as jnp
from jax import lax
from jax.experimental import pallas as pl
from jax.experimental.pallas import tpu as pltpu
from jax.sharding import PartitionSpec as P

GROUPS = 32
EPS = 1e-05
LANES = 128
MESH = pl.DeviceIdType.MESH
F32 = jnp.float32
BF16 = jnp.bfloat16
HIGHEST = lax.Precision.HIGHEST


def silu(v):
    half = 0.5 * v
    return half + half * jnp.tanh(half)


def lane_roll(v, shift):
    shift = shift % LANES
    return v if shift == 0 else pltpu.roll(v, shift, v.ndim - 1)


def place_lanes(pieces, width):
    if len(pieces) == 1:
        return pieces[0]
    block = lax.broadcasted_iota(jnp.int32, pieces[0].shape, pieces[0].ndim - 1) // width
    out = pieces[-1]
    for i in range(len(pieces) - 2, -1, -1):
        out = jnp.where(block == i, pieces[i], out)
    return out


def block_kernel(
    sizes,
    frames_ref, counts_ref, k1_ref, k2_ref, g1_ref, o1_ref, b1_ref, g2_ref, o2_ref, b2_ref,
    out_ref,
    xraw, xn, k1v, k2v, pk, part, zsend, zrecv, csend, rret,
    local_sem, gs_sem, gr_sem, fs_sem, zs_sem, zr_sem, as_sem, ar_sem,
):
    G, S, F, H, W, C, wo, npad, pack, hp = sizes
    g = lax.axis_index("span")
    me = lax.axis_index("space")
    core = me % 2
    chip = me // 2
    chips = S // 2
    sib = chip * 2 + (1 - core)
    cols = C // LANES
    cpg = C // GROUPS

    def ident(dev):
        return (g, dev)

    for i, (src, dst) in enumerate(((k1_ref, k1v), (k2_ref, k2v))):
        pltpu.make_async_copy(src, dst.at[:, 0:3 * wo], local_sem.at[i]).start()
    own = pltpu.make_async_copy(frames_ref, xraw.at[me], local_sem.at[2])
    own.start()

    zrecv[...] = jnp.zeros_like(zrecv)

    barrier = pltpu.get_barrier_semaphore()
    for k in range(1, S):
        pl.semaphore_signal(barrier, inc=1, device_id=ident((me + k) % S), device_id_type=MESH)
    for hop in (-2, -1, 1, 2):
        @pl.when((g + hop >= 0) & (g + hop < G))
        def _():
            pl.semaphore_signal(barrier, inc=1, device_id=(g + hop, me), device_id_type=MESH)
    others = jnp.minimum(g, 2) + jnp.minimum(G - 1 - g, 2)
    pl.semaphore_wait(barrier, S - 1 + others)

    def gather_copy(stage, src, buf, slot, dev, sem_at):
        return pltpu.make_async_remote_copy(
            src_ref=src, dst_ref=buf.at[slot],
            send_sem=gs_sem.at[stage, sem_at], recv_sem=gr_sem.at[stage, slot],
            device_id=ident(dev), device_id_type=MESH,
        )

    def gather_start(stage, src, buf):
        copies = []
        for k in range(1, chips):
            q = (chip + k) % chips
            copies.append(gather_copy(stage, src, buf, me, q * 2 + core, k))
        copies.append(gather_copy(stage, src, buf, me, sib, 0))
        for c in copies:
            c.start()
        return copies

    def gather_finish(stage, buf, copies, visit):
        def await_slot(slot):
            gather_copy(stage, buf.at[slot], buf, slot, sib, 0).wait_recv()

        await_slot(sib)
        visit(sib)
        forwards = []
        for k in range(1, chips):
            slot = ((chip + k) % chips) * 2 + core
            await_slot(slot)
            c = pltpu.make_async_remote_copy(
                src_ref=buf.at[slot], dst_ref=buf.at[slot],
                send_sem=fs_sem.at[stage, k], recv_sem=gr_sem.at[stage, slot],
                device_id=ident(sib), device_id_type=MESH,
            )
            c.start()
            forwards.append(c)
            visit(slot)
        for k in range(1, chips):
            slot = ((chip + k) % chips) * 2 + (1 - core)
            await_slot(slot)
            visit(slot)
        for c in copies + forwards:
            c.wait_send()

    copies = gather_start(0, frames_ref, xraw)

    xn[:, 0] = jnp.zeros((F, W, C), BF16)
    xn[:, H + 1] = jnp.zeros((F, W, C), BF16)
    if npad > 3 * wo:
        for dst in (k1v, k2v):
            dst[:, 3 * wo:npad] = jnp.zeros((9, npad - 3 * wo, C), BF16)

    count = counts_ref[g]
    own.wait()

    part[...] = jnp.zeros_like(part)

    def visit_row(slot):
        for f in range(F):
            v = xraw[slot, f].astype(F32).reshape(W // 8, 8, C)
            part[0, f] += jnp.sum(v, axis=0)
            part[1, f] += jnp.sum(v * v, axis=0)

    visit_row(me)
    gather_finish(0, xraw, copies, visit_row)

    members = float(H * W * cpg)
    row_id = lax.broadcasted_iota(jnp.int32, (LANES, LANES), 0)
    col_id = lax.broadcasted_iota(jnp.int32, (LANES, LANES), 1)

    def wide(ref):
        return jnp.concatenate([ref[j:j + 1, :] for j in range(cols)], axis=1)

    stats = jnp.concatenate(
        [jnp.sum(part[i, f], axis=0, keepdims=True) for i in range(2) for f in range(F)]
        + [jnp.zeros((8 - 2 * F, C), F32)], axis=0)
    tall = jnp.concatenate([stats[:, j * LANES:(j + 1) * LANES] for j in range(cols)], axis=0)
    same = (row_id // cpg == col_id // cpg).astype(F32)
    tall = jnp.dot(tall, same, precision=HIGHEST, preferred_element_type=F32)
    stats = jnp.concatenate([tall[j * 8:(j + 1) * 8] for j in range(cols)], axis=1) / members
    gain1 = wide(g1_ref)
    offset1 = wide(o1_ref)
    scales, shifts = [], []
    for f in range(F):
        average = stats[f:f + 1]
        spread = stats[F + f:F + f + 1] - average * average
        live = jnp.where(f < count, 1.0, 0.0)
        scale = lax.rsqrt(spread + EPS) * gain1
        scales.append(scale * live)
        shifts.append((offset1 - average * scale) * live)

    def norm_row(s, carry):
        for f in range(F):
            v = xraw[s, f].astype(F32)
            xn[f, 1 + s] = silu(v * scales[f] + shifts[f]).astype(BF16)
        return carry

    lax.fori_loop(0, S, norm_row, 0)

    tile = (me * wo) // LANES
    base = (me * wo) % LANES
    lane = lax.broadcasted_iota(jnp.int32, (1, LANES), 1)

    def own_lanes(ref):
        v = ref[pl.ds(tile, 1), :]
        v = jnp.where((lane >= base) & (lane < base + wo), v, 0.0)
        out = v
        for i in range(1, pack):
            out = out + lane_roll(v, i * wo)
        return out

    HW = H * W
    xpos = lax.broadcasted_iota(jnp.int32, (HW, LANES), 0) % W

    def packed(total):
        moved = []
        for j in range(3):
            at = (j * wo) // LANES * LANES
            t = total[:, at:at + LANES]
            if j == 0:
                t = jnp.where(xpos == 0, 0.0, pltpu.roll(t, 1, 0))
            elif j == 2:
                t = jnp.where(xpos == W - 1, 0.0, pltpu.roll(t, HW - 1, 0))
            moved.append(t)
        rows = HW // pack
        chunks = []
        for c in range(pack):
            acc = None
            for j in range(3):
                t = lane_roll(moved[j][c * rows:(c + 1) * rows], (c - j) * wo)
                acc = t if acc is None else acc + t
            chunks.append(acc)
        return place_lanes(chunks, wo)

    def taps(kv, dt):
        acc = None
        for dy in range(3):
            x = xn[:, dy:dy + H].reshape(F * HW, C)
            t = lax.dot_general(x, kv[dt * 3 + dy], (((1,), (1,)), ((), ())),
                                preferred_element_type=F32)
            acc = t if acc is None else acc + t
        return [acc[f * HW:(f + 1) * HW] for f in range(F)]

    def z_copies(stage):
        near = pltpu.make_async_remote_copy(
            src_ref=zsend.at[stage], dst_ref=zrecv.at[stage, 0:2],
            send_sem=zs_sem.at[stage, 0], recv_sem=zr_sem.at[stage, 0],
            device_id=(g + 1, me), device_id_type=MESH)
        far = pltpu.make_async_remote_copy(
            src_ref=zsend.at[stage, 1], dst_ref=zrecv.at[stage, 2],
            send_sem=zs_sem.at[stage, 1], recv_sem=zr_sem.at[stage, 1],
            device_id=(g + 2, me), device_id_type=MESH)
        return near, far

    def conv(stage, kv, bias):
        t0 = taps(kv, 0)
        t1 = taps(kv, 1)
        last0, last1 = t0[0], t1[0]
        second = jnp.zeros_like(t0[0])
        for f in range(1, F):
            last0 = jnp.where(f < count, t0[f], last0)
            last1 = jnp.where(f < count, t1[f], last1)
            second = jnp.where(f < count, t0[f - 1], second)
        zsend[stage, 0] = packed(last1 + second)
        zsend[stage, 1] = packed(last0)
        near, far = z_copies(stage)

        @pl.when(g + 1 < G)
        def _():
            near.start()

        @pl.when(g + 2 < G)
        def _():
            far.start()

        t2 = taps(kv, 2)
        outs = []
        for f in range(F):
            total = t2[f]
            if f >= 1:
                total = total + t1[f - 1]
            if f >= 2:
                total = total + t0[f - 2]
            outs.append(packed(total) + bias)

        @pl.when(g >= 1)
        def _():
            near.wait_recv()

        @pl.when(g >= 2)
        def _():
            far.wait_recv()

        alone = counts_ref[jnp.maximum(g - 1, 0)] < 2
        outs[0] = outs[0] + zrecv[stage, 0] + jnp.where(alone, zrecv[stage, 2], 0.0)
        outs[1] = outs[1] + zrecv[stage, 1]

        @pl.when(g + 1 < G)
        def _():
            near.wait_send()

        @pl.when(g + 2 < G)
        def _():
            far.wait_send()

        return [o.astype(BF16) for o in outs]

    pltpu.make_async_copy(k1_ref, k1v.at[:, 0:3 * wo], local_sem.at[0]).wait()
    conv1 = conv(0, k1v, own_lanes(b1_ref))

    wide1 = [v.astype(F32) for v in conv1]
    stats = jnp.concatenate(
        [jnp.sum(v, axis=0, keepdims=True) for v in wide1]
        + [jnp.sum(v * v, axis=0, keepdims=True) for v in wide1]
        + [jnp.zeros((8 - 2 * F, LANES), F32)], axis=0)
    same = ((row_id % wo) // cpg == (col_id % wo) // cpg).astype(F32)
    stats = jnp.dot(stats, same, precision=HIGHEST, preferred_element_type=F32) / members
    gain2 = own_lanes(g2_ref)
    offset2 = own_lanes(o2_ref)
    for f in range(F):
        average = stats[f:f + 1]
        spread = stats[F + f:F + f + 1] - average * average
        live = jnp.where(f < count, 1.0, 0.0)
        scale = lax.rsqrt(spread + EPS) * gain2
        shift = offset2 - average * scale
        pk[me, f] = silu(wide1[f] * (scale * live) + shift * live).astype(BF16)

    copies = gather_start(1, pk.at[me], pk)
    gather_finish(1, pk, copies, lambda slot: None)

    for j in range(cols):
        for f in range(F):
            loaded = [pk[j * pack + i, f].astype(F32) for i in range(pack)]
            for c in range(pack):
                v = place_lanes([lane_roll(loaded[i], (i - c) * wo) for i in range(pack)], wo)
                xn[f, 1 + c * hp:1 + (c + 1) * hp, :, j * LANES:(j + 1) * LANES] = (
                    v.astype(BF16).reshape(hp, W, LANES))

    pltpu.make_async_copy(k2_ref, k2v.at[:, 0:3 * wo], local_sem.at[1]).wait()
    conv2 = conv(1, k2v, own_lanes(b2_ref))
    for f in range(F):
        csend[:, f] = conv2[f].reshape(hp, W, LANES)

    def row_copy(dev, slot, k):
        return pltpu.make_async_remote_copy(
            src_ref=csend.at[dev % hp], dst_ref=rret.at[slot],
            send_sem=as_sem.at[k], recv_sem=ar_sem.at[slot],
            device_id=ident(dev), device_id_type=MESH)

    sends = [row_copy((me + k) % S, me, k) for k in range(1, S)]
    for c in sends:
        c.start()
    rret[me] = csend[me % hp]
    for k in range(1, S):
        row_copy((me + k) % S, (me + k) % S, k).wait_recv()
    chunk = me // hp
    for j in range(cols):
        pieces = [
            pltpu.roll(rret[j * pack + i].astype(F32).reshape(F * W, LANES),
                       ((i - chunk + pack) % pack) * wo, 1)
            for i in range(pack)
        ]
        out_ref[:, :, j * LANES:(j + 1) * LANES] = (
            place_lanes(pieces, wo).astype(BF16).reshape(F, W, LANES))
    for c in sends:
        c.wait_send()


def per_device(G, S, frames, counts, gain_one, offset_one, kernel_one, bias_one,
               gain_two, offset_two, kernel_two, bias_two):
    F, rows, W, C = frames.shape
    wo = kernel_one.shape[3]
    H = rows * S
    pack = LANES // wo
    hp = H // pack
    npad = -(-3 * wo // LANES) * LANES
    sizes = (G, S, F, H, W, C, wo, npad, pack, hp)
    live = (jnp.arange(F) < lax.dynamic_index_in_dim(
        counts, lax.axis_index("span"), keepdims=False)).astype(F32)

    def vec(v):
        return v.reshape(C // LANES, LANES)

    vmem = pl.BlockSpec(memory_space=pltpu.VMEM)
    hbm = pl.BlockSpec(memory_space=pl.ANY)
    returned = pl.pallas_call(
        functools.partial(block_kernel, sizes),
        out_shape=jax.ShapeDtypeStruct((F, W, C), BF16),
        in_specs=[hbm, pl.BlockSpec(memory_space=pltpu.SMEM), hbm, hbm] + [vmem] * 6,
        out_specs=vmem,
        scratch_shapes=[
            pltpu.VMEM((S, F, W, C), BF16),
            pltpu.VMEM((F, H + 2, W, C), BF16),
            pltpu.VMEM((9, npad, C), BF16),
            pltpu.VMEM((9, npad, C), BF16),
            pltpu.VMEM((S, F, hp * W, LANES), BF16),
            pltpu.VMEM((2, F, 8, C), F32),
            pltpu.VMEM((2, 2, hp * W, LANES), F32),
            pltpu.VMEM((2, 3, hp * W, LANES), F32),
            pltpu.VMEM((hp, F, W, LANES), BF16),
            pltpu.VMEM((S, F, W, LANES), BF16),
            pltpu.SemaphoreType.DMA((3,)),
            pltpu.SemaphoreType.DMA((2, S // 2)),
            pltpu.SemaphoreType.DMA((2, S)),
            pltpu.SemaphoreType.DMA((2, S // 2)),
            pltpu.SemaphoreType.DMA((2, 2)),
            pltpu.SemaphoreType.DMA((2, 2)),
            pltpu.SemaphoreType.DMA((S,)),
            pltpu.SemaphoreType.DMA((S,)),
        ],
        compiler_params=pltpu.CompilerParams(
            collective_id=0, has_side_effects=True, vmem_limit_bytes=56 * 1024 * 1024),
    )(
        frames.reshape(F, W, C), counts,
        kernel_one.reshape(9, 3 * wo, C), kernel_two.reshape(9, 3 * wo, C),
        vec(gain_one), vec(offset_one), vec(bias_one),
        vec(gain_two), vec(offset_two), vec(bias_two),
    )
    decoded = (frames.astype(F32) + returned.reshape(frames.shape).astype(F32)) * (
        live[:, None, None, None])
    return decoded.astype(BF16)


def solution(mesh):
    body = functools.partial(per_device, mesh.shape["span"], mesh.shape["space"])
    return jax.shard_map(
        body,
        mesh=mesh,
        in_specs=(
            P("span", "space", None, None), P(), P(), P(),
            P(None, None, None, "space", None), P(), P(), P(),
            P(None, None, None, "space", None), P(),
        ),
        out_specs=P("span", "space", None, None),
        check_vma=False,
    )
```

time: 181 us -> 46.2 us (0.26); the launches traced: 179 us -> 46 us
  waiting for transfers between devices: 60.7 us -> 0 us
  blocking collectives: 60 us -> 0 us
  Pallas kernels: 0 us -> 42.4 us
  between operations: 16.3 us -> 0.03 us
  matrix products: 13.3 us -> 0 us
  local copies, waits for them, and re-layouts: 12.3 us -> 1.24 us
  other arithmetic: 7.91 us -> 2.26 us
  loops' own time: 4.51 us -> 0 us
  starting transfers between devices: 3.5 us -> 0 us
    all_gather x2 -> x0, waiting for transfers between devices: 56.4 us -> none  [the longest x1 29.4 us: per_device(): full_one = lax.all_gather(stacked_one, 'space', axis=1, tiled=True)]
    pallas_call x0 -> x1, Pallas kernels: none -> 42.4 us  [per_device(): pl.pallas_call(functools.partial(block_kernel, sizes), out_shape=jax.Shap...]
    psum x2 -> x0, blocking collectives: 23.9 us -> none  [the longest x1 12.1 us: per_device(): total_two, squares_two = lax.psum((total_two, squares_two), 'space')]
    all_gather x2 -> x0, blocking collectives: 22.6 us -> none  [entering(): gathered = jax.tree.map(lambda a: lax.all_gather(a, axis), part)]
    dot_general x6 -> x0, matrix products: 13.3 us -> none  [spread_taps(): lax.dot_general(window.reshape(-1, channels), matrix, (((1,), (1,)), ((),...]
    all_to_all x1 -> x0, blocking collectives: 7.04 us -> none  [per_device(): lax.all_to_all(conv_two, 'space', split_axis=1, concat_axis=3, tiled=True)]
    unnamed x1 -> x0, blocking collectives: 6.36 us -> none
    dynamic_slice x11 -> x1, local copies, waits for them, and re-layouts: 6.71 us -> 1.24 us  [per_device(): lax.dynamic_index_in_dim(counts, lax.axis_index('span'), keepdims=False)]
  transfers between devices with their start and end apart: 3 -> 0, of which waited for: 3 -> 0; matrix products, arithmetic and copies ran while one was open for 1% -> 0% of each run, Pallas kernels for 0% -> 0%
where the time goes in v1:
time: 46.2 us; the launch traced here: 46 us
  Pallas kernels  42.4 us (92%)
  other arithmetic  2.26 us (5%)
  local copies, waits for them, and re-layouts  1.24 us (3%)
    pallas_call x1, Pallas kernels, per_device(): pl.pallas_call(functools.partial(block_kernel, sizes), out_shape=jax.Shap...  42.4 us
    convert_element_type x1, other arithmetic, per_device(): return decoded.astype(BF16)  1.61 us
    dynamic_slice x1, local copies, waits for them, and re-layouts, per_device(): lax.dynamic_index_in_dim(counts, lax.axis_index('span'), keepdims=False)  1.24 us

profile of v1, /device:TPU:25, one launch (start us, length us, event | category | flops | bytes accessed | tf_op | source)
XLA Modules:
  0.0 46.0 jit_solution(14278870173538466255)
XLA Ops:
  0.0 1.2 %dynamic_slice.4 = s32[1]{0:T(128)} dynamic-slice(s32[4]{0:T(128)} %counts_ref.1, s32[]{:T(128)S(6)} %select_n.4), dynamic_slice_sizes={1} | dynamic-slice | bytes 12 | tf_op jit(solution)/shard_map/jit(dynamic_index_in_dim)/dynamic_slice | solution.py:351
  1.2 0.6 %compare_convert_fusion = f32[3]{0:T(128)S(1)} fusion(s32[]{:T(128)} %bitcast.11), kind=kLoop, calls=%fused_computation.4 | loop fusion | flops 6 | bytes 16 | tf_op jit(solution)/shard_map/convert_element_type | solution.py:352
  1.9 0.0 copy-start
  1.9 42.4 %shard_map.100 = bf16[3,32,512]{2,1,0:T(8,128)(2,1)} custom-call(bf16[3,32,512]{2,1,0:T(8,128)(2,1)} %bitcast.19, s32[4]{0:T(128)} %counts_ref.1, bf16[9,192,512]{2,1,0:T(8,128)(2,1)} %bitcast.17, bf16[9,192,512]{2,1,0:T(8,128)(2,1)} %bitcast.18, f32[4,128]{1,0:T(4,128)} %bitcast.20, f32[4,128]{1,0:T(4,128)} %bitcast.21, f32[4,128]{1,0:T(4,128)} %bitcast.22, ...), custom_call_target="tpu_custom_call" | custom-call | tf_op jit(solution)/shard_map/pallas_call | solution.py:359
  44.4 0.0 copy-done
  44.4 1.6 %fusion.2 = bf16[3,1,32,512]{3,2,1,0:T(8,128)(2,1)} fusion(bf16[3,32,512]{2,1,0:T(8,128)(2,1)} %shard_map.100, bf16[3,1,32,512]{3,2,1,0:T(8,128)(2,1)S(1)} %copy-done, f32[3]{0:T(128)S(1)} %compare_convert_fusion), kind=kLoop, calls=%fused_computation.3 | loop fusion | flops 245760 | bytes 294924 | tf_op jit(solution)/shard_map/convert_element_type | solution.py:394
Async XLA Ops:
  1.9 42.5 %copy-start = (bf16[3,1,32,512]{3,2,1,0:T(8,128)(2,1)S(1)}, bf16[3,1,32,512]{3,2,1,0:T(8,128)(2,1)}, u32[]{:S(2)}) copy-start(bf16[3,1,32,512]{3,2,1,0:T(8,128)(2,1)} %param.10) | copy-start | bytes 294916

commit v2 on v1

v2 whole, which is shorter than its diff:
```python
import functools

import jax
import jax.numpy as jnp
from jax import lax
from jax.experimental import pallas as pl
from jax.experimental.pallas import tpu as pltpu
from jax.sharding import PartitionSpec as P

GROUPS = 32
EPS = 1e-05
LANES = 128
MESH = pl.DeviceIdType.MESH
F32 = jnp.float32
BF16 = jnp.bfloat16
HIGHEST = lax.Precision.HIGHEST


def silu(v):
    half = 0.5 * v
    return half + half * jnp.tanh(half)


def lane_roll(v, shift):
    shift = shift % LANES
    return v if shift == 0 else pltpu.roll(v, shift, v.ndim - 1)


def place_lanes(pieces, width):
    if len(pieces) == 1:
        return pieces[0]
    block = lax.broadcasted_iota(jnp.int32, pieces[0].shape, pieces[0].ndim - 1) // width
    out = pieces[-1]
    for i in range(len(pieces) - 2, -1, -1):
        out = jnp.where(block == i, pieces[i], out)
    return out


def block_kernel(
    sizes,
    frames_ref, counts_ref, k1_ref, k2_ref, g1_ref, o1_ref, b1_ref, g2_ref, o2_ref, b2_ref,
    out_ref,
    xown, xraw, xn, k1v, k2v, pk, zsend, zrecv, csend, rret,
    local_sem, gs_sem, gr_sem, fs_sem, zs_sem, zr_sem, as_sem, ar_sem,
):
    G, S, F, H, W, C, wo, npad, pack, hp = sizes
    g = lax.axis_index("span")
    me = lax.axis_index("space")
    core = me % 2
    chip = me // 2
    chips = S // 2
    sib = chip * 2 + (1 - core)
    cols = C // LANES
    cpg = C // GROUPS
    HW = H * W
    wq = W // pack

    def ident(dev):
        return (g, dev)

    own = pltpu.make_async_copy(frames_ref, xown, local_sem.at[2])
    own.start()
    weights = [
        pltpu.make_async_copy(src, dst.at[:, 0:3 * wo], local_sem.at[i])
        for i, (src, dst) in enumerate(((k1_ref, k1v), (k2_ref, k2v)))
    ]
    for w in weights:
        w.start()

    barrier = pltpu.get_barrier_semaphore()
    zrecv[...] = jnp.zeros_like(zrecv)
    for k in range(1, S):
        pl.semaphore_signal(barrier, inc=1, device_id=ident((me + k) % S), device_id_type=MESH)
    for hop in (-2, -1, 1, 2):
        @pl.when((g + hop >= 0) & (g + hop < G))
        def _():
            pl.semaphore_signal(barrier, inc=1, device_id=(g + hop, me), device_id_type=MESH)

    count = counts_ref[g]
    own.wait()
    for p in range(F):
        xraw[p, me] = xown[jnp.maximum(count - 1 - p, 0)]

    xn[:, 0] = jnp.zeros((F, W, C), BF16)
    xn[:, H + 1] = jnp.zeros((F, W, C), BF16)
    if npad > 3 * wo:
        for dst in (k1v, k2v):
            dst[:, 3 * wo:npad] = jnp.zeros((9, npad - 3 * wo, C), BF16)

    others = jnp.minimum(g, 2) + jnp.minimum(G - 1 - g, 2)
    pl.semaphore_wait(barrier, S - 1 + others)

    def peer(k):
        if chips % 2:
            return (chip + k) % chips
        return ((chip // 2 + k // 2) % (chips // 2)) * 2 + (chip % 2 + k % 2) % 2

    order = list(range(chips - 1, 0, -1))

    def block_copy(stage, buf, p, slot, dev, send):
        return pltpu.make_async_remote_copy(
            src_ref=buf.at[p, slot], dst_ref=buf.at[p, slot],
            send_sem=send, recv_sem=gr_sem.at[stage, p, slot],
            device_id=ident(dev), device_id_type=MESH,
        )

    def piece_start(stage, buf, p):
        copies = [
            block_copy(stage, buf, p, me, peer(k) * 2 + core, gs_sem.at[stage, p, k])
            for k in order
        ] + [block_copy(stage, buf, p, me, sib, gs_sem.at[stage, p, 0])]
        for c in copies:
            c.start()
        return copies

    def piece_finish(stage, buf, p):
        def await_slot(slot):
            block_copy(stage, buf, p, slot, sib, gs_sem.at[stage, p, 0]).wait_recv()

        forwards = []
        for k in reversed(order):
            slot = peer(k) * 2 + core
            await_slot(slot)
            c = block_copy(stage, buf, p, slot, sib, fs_sem.at[stage, p, k])
            c.start()
            forwards.append(c)
        await_slot(sib)
        for k in reversed(order):
            await_slot(peer(k) * 2 + (1 - core))
        return forwards

    started = []
    for p in range(F):
        started += piece_start(0, xraw, p)

    members = float(H * W * cpg)
    row_id = lax.broadcasted_iota(jnp.int32, (LANES, LANES), 0)
    col_id = lax.broadcasted_iota(jnp.int32, (LANES, LANES), 1)
    same_one = (row_id // cpg == col_id // cpg).astype(F32)
    same_two = ((row_id % wo) // cpg == (col_id % wo) // cpg).astype(F32)

    def wide(ref):
        return jnp.concatenate([ref[j:j + 1, :] for j in range(cols)], axis=1)

    gain1 = wide(g1_ref)
    offset1 = wide(o1_ref)

    tile = (me * wo) // LANES
    base = (me * wo) % LANES
    lane = lax.broadcasted_iota(jnp.int32, (1, LANES), 1)

    def own_lanes(ref):
        v = ref[pl.ds(tile, 1), :]
        v = jnp.where((lane >= base) & (lane < base + wo), v, 0.0)
        out = v
        for i in range(1, pack):
            out = out + lane_roll(v, i * wo)
        return out

    bias1, bias2 = own_lanes(b1_ref), own_lanes(b2_ref)
    gain2, offset2 = own_lanes(g2_ref), own_lanes(o2_ref)

    xpos = lax.broadcasted_iota(jnp.int32, (HW, LANES), 0) % W

    def norm_terms(sums, squares, gain, offset, p):
        average = sums / members
        spread = squares / members - average * average
        live = jnp.where(p < count, 1.0, 0.0)
        scale = lax.rsqrt(spread + EPS) * gain
        return scale * live, (offset - average * scale) * live

    def norm_one(p):
        def add_row(s, carry):
            v = xraw[p, s].astype(F32).reshape(W // 8, 8, C)
            return carry[0] + jnp.sum(v, axis=0), carry[1] + jnp.sum(v * v, axis=0)

        zero = jnp.zeros((8, C), F32)
        sums, squares = lax.fori_loop(0, S, add_row, (zero, zero), unroll=True)
        tall = jnp.concatenate(
            [t[:, j * LANES:(j + 1) * LANES] for t in (sums, squares) for j in range(cols)], axis=0)
        tall = jnp.sum(tall.reshape(2 * cols, 8, LANES), axis=1)
        tall = jnp.dot(tall, same_one, precision=HIGHEST, preferred_element_type=F32)
        sums = jnp.concatenate([tall[j:j + 1] for j in range(cols)], axis=1)
        squares = jnp.concatenate([tall[cols + j:cols + j + 1] for j in range(cols)], axis=1)
        scale, shift = norm_terms(sums, squares, gain1, offset1, p)

        def norm_row(s, carry):
            v = xraw[p, s].astype(F32)
            xn[p, 1 + s] = silu(v * scale + shift).astype(BF16)
            return carry

        lax.fori_loop(0, S, norm_row, 0, unroll=True)

    def unpack(p):
        for j in range(cols):
            loaded = [pk[p, j * pack + i].astype(F32) for i in range(pack)]
            for c in range(pack):
                v = place_lanes([lane_roll(loaded[i], (i - c) * wo) for i in range(pack)], wo)
                xn[p, 1 + c * hp:1 + (c + 1) * hp, :, j * LANES:(j + 1) * LANES] = (
                    v.astype(BF16).reshape(hp, W, LANES))

    def packed(total):
        moved = []
        for j in range(3):
            at = (j * wo) // LANES * LANES
            t = total[:, at:at + LANES]
            if j == 0:
                t = jnp.where(xpos == 0, 0.0, pltpu.roll(t, 1, 0))
            elif j == 2:
                t = jnp.where(xpos == W - 1, 0.0, pltpu.roll(t, HW - 1, 0))
            moved.append(t)
        rows = HW // pack
        chunks = []
        for c in range(pack):
            acc = None
            for j in range(3):
                t = lane_roll(moved[j][c * rows:(c + 1) * rows], (c - j) * wo)
                acc = t if acc is None else acc + t
            chunks.append(acc)
        return place_lanes(chunks, wo)

    def taps(kv, dt, p):
        acc = None
        for dy in range(3):
            x = xn[p, dy:dy + H].reshape(HW, C)
            t = lax.dot_general(x, kv[dt * 3 + dy], (((1,), (1,)), ((), ())),
                                preferred_element_type=F32)
            acc = t if acc is None else acc + t
        return acc

    def z_copy(stage, which):
        src, hop = ((0, 1), (1, 1), (1, 2))[which]
        return pltpu.make_async_remote_copy(
            src_ref=zsend.at[stage, src], dst_ref=zrecv.at[stage, which],
            send_sem=zs_sem.at[stage, which], recv_sem=zr_sem.at[stage, which],
            device_id=(g + hop, me), device_id_type=MESH)

    def z_start(stage, which):
        hop = (1, 1, 2)[which]

        @pl.when(g + hop < G)
        def _():
            z_copy(stage, which).start()

    def conv(stage, buf, kv, bias, prepare, emit):
        started = []
        sums = [None] * F
        near = None
        for p in range(F):
            started += piece_finish(stage, buf, p)
            prepare(p)
            if p == 0:
                weights[stage].wait()
                zsend[stage, 1] = packed(taps(kv, 0, 0))
                z_start(stage, 2)
                z_start(stage, 1)
                near = taps(kv, 1, 0)
            elif p == 1:
                t = taps(kv, 0, 1)
                zsend[stage, 0] = packed(near + t)
                z_start(stage, 0)
            for at in range(max(p - 2, 0), p + 1):
                dt = 2 - (p - at)
                t = taps(kv, dt, p)
                sums[at] = t if sums[at] is None else sums[at] + t
                if p == F - 1:
                    if at == 0:
                        for which, hop in ((1, 1), (2, 2), (0, 1)):
                            @pl.when(g >= hop)
                            def _():
                                z_copy(stage, which).wait_recv()
                        alone = counts_ref[jnp.maximum(g - 1, 0)] < 2
                        first = zrecv[stage, 0] + jnp.where(alone, zrecv[stage, 2], 0.0)
                        later = zrecv[stage, 1]
                    frame = count - 1 - at
                    cross = jnp.where(frame == 0, first, jnp.where(frame == 1, later, 0.0))
                    emit(at, (packed(sums[at]) + cross + bias).astype(BF16))
        for which, hop in ((1, 1), (2, 2), (0, 1)):
            @pl.when(g + hop < G)
            def _():
                z_copy(stage, which).wait_send()
        return started

    def norm_two(p, v):
        v = v.astype(F32)
        stats = jnp.concatenate(
            [jnp.sum(v, axis=0, keepdims=True), jnp.sum(v * v, axis=0, keepdims=True),
             jnp.zeros((6, LANES), F32)], axis=0)
        stats = jnp.dot(stats, same_two, precision=HIGHEST, preferred_element_type=F32)
        scale, shift = norm_terms(stats[0:1], stats[1:2], gain2, offset2, p)
        pk[p, me] = silu(v * scale + shift).astype(BF16)
        started.extend(piece_start(1, pk, p))

    started += conv(0, xraw, k1v, bias1, norm_one, norm_two)

    narrow = wq % 16 == 0

    def row_out(p, v):
        if not narrow:
            csend[:, p] = v.reshape(hp, W, LANES)
            return
        v = v.astype(F32)
        for d in range(S):
            c, r = d // hp, d % hp
            parts = [
                lane_roll(v[r * W + h * wq:r * W + (h + 1) * wq], (h - c) * wo)
                for h in range(pack)
            ]
            csend[d, p] = place_lanes(parts, wo).astype(BF16)

    started += conv(1, pk, k2v, bias2, unpack, row_out)

    def row_copy(dev, slot, k):
        return pltpu.make_async_remote_copy(
            src_ref=csend.at[dev if narrow else dev % hp], dst_ref=rret.at[slot],
            send_sem=as_sem.at[k], recv_sem=ar_sem.at[slot],
            device_id=ident(dev), device_id_type=MESH)

    sends = [row_copy((me + k) % S, me, k) for k in range(1, S)]
    for c in sends:
        c.start()
    rret[me] = csend[me if narrow else me % hp]
    for c in started:
        c.wait_send()
    for k in range(1, S):
        row_copy((me + k) % S, (me + k) % S, k).wait_recv()
    chunk = me // hp
    for j in range(cols):
        if narrow:
            got = [rret[j * pack + i].astype(F32).reshape(F * wq, LANES) for i in range(pack)]
            tiles = [
                place_lanes([lane_roll(got[i], (i - h) * wo) for i in range(pack)], wo)
                .reshape(F, wq, LANES)
                for h in range(pack)
            ]
            moved = [jnp.concatenate([t[p] for t in tiles], axis=0) for p in range(F)]
        else:
            got = place_lanes([
                pltpu.roll(rret[j * pack + i].astype(F32).reshape(F * W, LANES),
                           ((i - chunk + pack) % pack) * wo, 1)
                for i in range(pack)
            ], wo).reshape(F, W, LANES)
            moved = [got[p] for p in range(F)]
        at = slice(j * LANES, (j + 1) * LANES)
        for f in range(F):
            v = moved[0]
            for p in range(1, F):
                v = jnp.where(count - 1 - f == p, moved[p], v)
            v = xown[f, :, at].astype(F32) + v
            out_ref[f, :, at] = jnp.where(f < count, v, 0.0).astype(BF16)
    for c in sends:
        c.wait_send()


def per_device(G, S, frames, counts, gain_one, offset_one, kernel_one, bias_one,
               gain_two, offset_two, kernel_two, bias_two):
    F, rows, W, C = frames.shape
    wo = kernel_one.shape[3]
    H = rows * S
    pack = LANES // wo
    hp = H // pack
    npad = -(-3 * wo // LANES) * LANES
    sizes = (G, S, F, H, W, C, wo, npad, pack, hp)
    if (W // pack) % 16 == 0:
        row_block = [(S, F, W // pack, LANES)] * 2
    else:
        row_block = [(hp, F, W, LANES), (S, F, W, LANES)]
    def vec(v):
        return v.reshape(C // LANES, LANES)

    vmem = pl.BlockSpec(memory_space=pltpu.VMEM)
    hbm = pl.BlockSpec(memory_space=pl.ANY)
    decoded = pl.pallas_call(
        functools.partial(block_kernel, sizes),
        out_shape=jax.ShapeDtypeStruct((F, W, C), BF16),
        in_specs=[hbm, pl.BlockSpec(memory_space=pltpu.SMEM), hbm, hbm] + [vmem] * 6,
        out_specs=vmem,
        scratch_shapes=[
            pltpu.VMEM((F, W, C), BF16),
            pltpu.VMEM((F, S, W, C), BF16),
            pltpu.VMEM((F, H + 2, W, C), BF16),
            pltpu.VMEM((9, npad, C), BF16),
            pltpu.VMEM((9, npad, C), BF16),
            pltpu.VMEM((F, S, hp * W, LANES), BF16),
            pltpu.VMEM((2, 2, hp * W, LANES), F32),
            pltpu.VMEM((2, 3, hp * W, LANES), F32),
            pltpu.VMEM(row_block[0], BF16),
            pltpu.VMEM(row_block[1], BF16),
            pltpu.SemaphoreType.DMA((3,)),
            pltpu.SemaphoreType.DMA((2, F, S // 2)),
            pltpu.SemaphoreType.DMA((2, F, S)),
            pltpu.SemaphoreType.DMA((2, F, S // 2)),
            pltpu.SemaphoreType.DMA((2, 3)),
            pltpu.SemaphoreType.DMA((2, 3)),
            pltpu.SemaphoreType.DMA((S,)),
            pltpu.SemaphoreType.DMA((S,)),
        ],
        compiler_params=pltpu.CompilerParams(
            collective_id=0, has_side_effects=True, vmem_limit_bytes=56 * 1024 * 1024),
    )(
        frames.reshape(F, W, C), counts,
        kernel_one.reshape(9, 3 * wo, C), kernel_two.reshape(9, 3 * wo, C),
        vec(gain_one), vec(offset_one), vec(bias_one),
        vec(gain_two), vec(offset_two), vec(bias_two),
    )
    return decoded.reshape(frames.shape)


def solution(mesh):
    body = functools.partial(per_device, mesh.shape["span"], mesh.shape["space"])
    return jax.shard_map(
        body,
        mesh=mesh,
        in_specs=(
            P("span", "space", None, None), P(), P(), P(),
            P(None, None, None, "space", None), P(), P(), P(),
            P(None, None, None, "space", None), P(),
        ),
        out_specs=P("span", "space", None, None),
        check_vma=False,
    )
```

time: 46.2 us -> 35.9 us (0.78)
  Pallas kernels: 42.4 us -> 34.2 us
  other arithmetic: 2.26 us -> 0 us
    pallas_call x1, Pallas kernels: 42.4 us -> 34.2 us  [per_device(): pl.pallas_call(functools.partial(block_kernel, sizes), out_shape=jax.Shap...]
    convert_element_type x2 -> x0, other arithmetic: 2.26 us -> none  [the longest x1 1.61 us: per_device(): return decoded.astype(BF16)]
    unnamed x2 -> x1, local copies, waits for them, and re-layouts: 0.01 us -> 1.54 us
    dynamic_slice x1 -> x0, local copies, waits for them, and re-layouts: 1.24 us -> none  [per_device(): lax.dynamic_index_in_dim(counts, lax.axis_index('span'), keepdims=False)]
where the time goes in v2:
time: 35.9 us; the launch traced here: 35.7 us
  Pallas kernels  34.2 us (95%)
  local copies, waits for them, and re-layouts  1.54 us (4%)
    pallas_call x1, Pallas kernels, per_device(): pl.pallas_call(functools.partial(block_kernel, sizes), out_shape=jax.Shap...  34.2 us
    unnamed x1, local copies, waits for them, and re-layouts  1.54 us

profile of v2, /device:TPU:25, one launch (start us, length us, event | category | flops | bytes accessed | tf_op | source)
XLA Modules:
  0.0 35.7 jit_solution(18174209089195715179)
XLA Ops:
  0.0 34.2 %shard_map.100 = bf16[3,32,512]{2,1,0:T(8,128)(2,1)} custom-call(bf16[3,32,512]{2,1,0:T(8,128)(2,1)} %bitcast.15, s32[4]{0:T(128)} %counts_ref.1, bf16[9,192,512]{2,1,0:T(8,128)(2,1)} %bitcast.12, bf16[9,192,512]{2,1,0:T(8,128)(2,1)} %bitcast.13, f32[4,128]{1,0:T(4,128)} %bitcast.16, f32[4,128]{1,0:T(4,128)} %bitcast.17, f32[4,128]{1,0:T(4,128)} %bitcast.18, ...), custom_call_target="tpu_custom_call" | custom-call | tf_op jit(solution)/shard_map/pallas_call | solution.py:373
  34.2 1.5 %copy.13 = bf16[3,1,32,512]{3,2,1,0:T(8,128)(2,1)} copy(bf16[3,1,32,512]{3,2,1,0:T(8,128)(2,1)} %bitcast.14) | data formatting | bytes 196608
